TPU v7x, 32 devices: a whole 2x2x4 slice. The times are simulated.
32 devices in a mesh: space: 4 (over z), orb: 8 (over y, x, core).
Axes of the slice: x: 2, y: 2, z: 4, core: 2. Of those that a mesh axis runs over, the one named last changes fastest.
Arguments:
- orbitals: bfloat16 [128, 40, 1600], P(('space', 'orb')), may hold values from -6 to 6
- box_offset: int32 [128, 3], replicated, may hold values from 0 to 79, as said below
- send_index: int32 [32, 2, 8], P(('space', 'orb')), may hold values from 0 to 3
- pair_left: int32 [32, 2, 8], P(('space', 'orb')), may hold values from 0 to 3
Outputs:
- exchange_field: float32 [128, 40, 1600], P(('space', 'orb'))
Inputs may be any that keep to these rules, and one draw needn't show every extreme that they name: `box_offset`: box corners are cell coordinates on the periodic grid of 80 cells a side.
All inputs are finite; a program needn't handle non-finite values.
Results may differ from a plain program's by a relative error of at most 0.0008.
Values may be sent and summed in bfloat16 or wider, within the bound.
No kernel may reach another device: no remote copies, remote signals or barrier semaphores. Data moves between devices by JAX's collectives and lax.ppermute only.
A program may use at most 128 MiB of HBM per device.

v0:
```python
import jax
import jax.numpy as jnp
from jax import lax
from jax.sharding import PartitionSpec as P

B = 40
ITERS = 4


screen_shift = 0.25
pair_block = 8


def passed_along(block, axis, distance):
    devices = range(lax.axis_size(axis))
    route = [((i - distance) % len(devices), i) for i in devices]
    return lax.ppermute(block, axis, route)


def apply_operator(values, box_side):
    row_pad = jnp.pad(values, ((0, 0), (1, 1), (0, 0)))
    summed = row_pad[:, 2:, :] + row_pad[:, :-2, :]
    flat_pad = jnp.pad(values, ((0, 0), (0, 0), (box_side, box_side)))
    summed = summed + flat_pad[:, :, 2 * box_side :] + flat_pad[:, :, : -2 * box_side]
    inner_pad = jnp.pad(values, ((0, 0), (0, 0), (1, 1)))
    column = lax.broadcasted_iota(jnp.int32, (1, 1, box_side * box_side), 2) % box_side
    next_cell = jnp.where(column < box_side - 1, inner_pad[:, :, 2:], 0.0)
    earlier = jnp.where(column > 0, inner_pad[:, :, :-2], 0.0)
    return (6.0 + screen_shift) * values - summed - next_cell - earlier


def solve_poisson(density, box_side):
    solution = jnp.zeros_like(density)
    residual = density
    direction = density
    norm_now = jnp.sum(residual * residual, axis=(1, 2), keepdims=True)
    for turn_index in range(ITERS):
        applied = apply_operator(direction, box_side)
        step_len = norm_now / jnp.sum(direction * applied, axis=(1, 2), keepdims=True)
        solution = solution + step_len * direction
        residual = residual - step_len * applied
        norm_next = jnp.sum(residual * residual, axis=(1, 2), keepdims=True)
        direction = residual + norm_next / norm_now * direction
        norm_now = norm_next
    return solution


def displace(box_values, displacement, box_side):
    half_side = box_side // 2
    flat_reach = half_side * box_side + half_side
    padded = jnp.pad(box_values, ((half_side, half_side), (flat_reach, flat_reach)))
    start_row = half_side - displacement[0]
    start_col = flat_reach - (displacement[1] * box_side + displacement[2])
    moved = lax.dynamic_slice(padded, (start_row, start_col), (box_side, box_side * box_side))
    column = lax.broadcasted_iota(jnp.int32, (1, box_side * box_side), 1) % box_side
    source_col = column - displacement[2]
    keep = (source_col >= 0) & (source_col < box_side)
    return jnp.where(keep, moved, jnp.zeros((), moved.dtype))


def pair_geometry(left_offset, right_offset, grid_cells, box_side):
    raw_gap = (right_offset - left_offset + grid_cells // 2) % grid_cells - grid_cells // 2
    displacement = jnp.clip(raw_gap, -(box_side // 2), box_side // 2)
    live_flag = jnp.all(raw_gap == displacement, axis=-1).astype(jnp.int32)
    return (displacement, live_flag)


def pair_terms(left_boxes, right_boxes, displacement, live_flag, box_side):
    shifted = jax.vmap(displace, in_axes=(0, 0, None))(right_boxes, displacement, box_side)
    shifted_wide = shifted.astype(jnp.float32)
    left_wide = left_boxes.astype(jnp.float32)
    potential = solve_poisson(left_wide * shifted_wide, box_side)
    weight = live_flag.astype(jnp.float32)[:, None, None]
    near_term = weight * potential * shifted_wide
    product = potential * left_wide
    far_term = weight * jax.vmap(displace, in_axes=(0, 0, None))(product, -displacement, box_side)
    return (near_term, far_term)


def collect_terms(indices, terms, local_count):
    picks = (indices[:, None] == jnp.arange(local_count, dtype=jnp.int32)[None, :]).astype(
        jnp.float32
    )
    flat_terms = terms.reshape(terms.shape[0], -1)
    return jnp.dot(
        picks.T, flat_terms, precision=lax.Precision.HIGHEST, preferred_element_type=jnp.float32
    )


def per_device(orbitals, box_offset, send_index, pair_left):
    box_side = B
    local_count = orbitals.shape[0]
    space_count = lax.axis_size("space")
    orb_count = lax.axis_size("orb")
    grid_cells = space_count * (box_side // 2)
    space_pos = lax.axis_index("space")
    orb_pos = lax.axis_index("orb")
    device = space_pos * orb_count + orb_pos
    sender_table = lax.all_gather(send_index, ("space", "orb"), axis=0, tiled=True)
    group_offset = jnp.arange(2, dtype=jnp.int32)[:, None]
    source_orb = jnp.arange(orb_count, dtype=jnp.int32)[None, :]
    source = (space_pos + group_offset) % space_count * orb_count + source_orb
    chosen = sender_table[source, jnp.broadcast_to(group_offset, source.shape), orb_pos]
    right_index = source * local_count + chosen
    left_local = pair_left[0]
    left_index = device * local_count + left_local
    displacement, live_flag = pair_geometry(
        box_offset[left_index], box_offset[right_index], grid_cells, box_side
    )
    members = lax.all_gather(orbitals, "orb", axis=0, tiled=True)
    following = passed_along(members, "space", -1)
    member_rows = source_orb[0] * local_count + chosen
    right_boxes = jnp.stack([members[member_rows[0]], following[member_rows[1]]])
    slot_total = 2 * orb_count
    left_flat = left_local.reshape(slot_total)
    left_boxes = orbitals[left_flat]
    right_boxes = right_boxes.reshape(slot_total, box_side, box_side * box_side)
    displacement = displacement.reshape(slot_total, 3)
    live_flag = live_flag.reshape(slot_total)
    block_count = slot_total // pair_block

    def run_block(block_data):
        return pair_terms(block_data[0], block_data[1], block_data[2], block_data[3], box_side)

    near_term, far_term = lax.map(
        run_block,
        (
            left_boxes.reshape(block_count, pair_block, box_side, box_side * box_side),
            right_boxes.reshape(block_count, pair_block, box_side, box_side * box_side),
            displacement.reshape(block_count, pair_block, 3),
            live_flag.reshape(block_count, pair_block),
        ),
    )
    near_term = near_term.reshape(slot_total, box_side, box_side * box_side)
    far_term = far_term.reshape(slot_total, box_side, box_side * box_side)
    far_term = far_term.reshape(2, orb_count, box_side, box_side * box_side)
    returned = lax.all_to_all(far_term, "orb", split_axis=1, concat_axis=1, tiled=True)
    behind = passed_along(returned[1].astype(jnp.bfloat16), "space", 1).astype(jnp.float32)
    back_terms = jnp.stack([returned[0], behind]).reshape(slot_total, box_side, box_side * box_side)
    exchange_field = collect_terms(left_flat, near_term, local_count) + collect_terms(
        send_index[0].reshape(slot_total), back_terms, local_count
    )
    return exchange_field.reshape(local_count, box_side, box_side * box_side)


def solution(mesh):
    in_specs = (
        P(("space", "orb"), None, None),
        P(),
        P(("space", "orb"), None, None),
        P(("space", "orb"), None, None),
    )
    out_specs = P(("space", "orb"), None, None)
    return jax.shard_map(
        per_device, mesh=mesh, in_specs=in_specs, out_specs=out_specs, check_vma=False
    )
```

profile of v0, /device:TPU:12, one launch (start us, length us, event | category | flops | bytes accessed | tf_op | source)
XLA Modules:
  0.0 472.9 jit_solution(16940764000908273934)
XLA Ops:
  7.3 40.0 %all-gather.2.cloned.1.call-done = bf16[32,40,1600]{2,1,0:T(8,128)(2,1)} async-done(((bf16[4,40,1600]{2,1,0:T(8,128)(2,1)}), bf16[32,40,1600]{2,1,0:T(8,128)(2,1)}) %all-gather.2.cloned.1.call-update) | async-done | bytes 4096016 | tf_op jit(solution)/shard_map/all_gather | solution.py:110
  47.9 119.3 %all_gather.6 = s32[32,2,8]{2,1,0:T(2,128)S(1)} all-gather(s32[1,2,8]{2,1,0:T(2,128)} %param.8), channel_id=1, replica_groups=mesh['space'=4,'orb'=8] {'space','orb'}, dimensions={0}, use_global_device_ids=true | all-gather | bytes 2112 | tf_op jit(solution)/shard_map/all_gather | solution.py:99
  175.8 3.9 gather_fusion.5
  182.5 182.1 %while.26 = (s32[]{:T(128)}, f32[2,8,40,1600]{3,2,1,0:T(8,128)}, f32[2,8,40,1600]{3,2,0,1:T(8,128)}, s32[2,8]{1,0:T(2,128)S(1)}, bf16[2,8,40,1600]{3,2,1,0:T(8,1...) while((s32[]{:T(128)}, f32[2,8,40,1600]{3,2,1,0:T(8,128)}, ...), condition=%wide.region_10.11_spmd.clone, body=%wide.region_1.10_spmd.sunk.clone | while | flops 47741088 | bytes 127858176 | solution.py:125
  187.0 29.5 %while.24 = (s32[]{:T(128)}, bf16[8,80,3240]{2,1,0:T(8,128)(2,1)}, s32[8,3]{0,1:T(4,128)S(1)}, bf16[8,40,1600]{2,1,0:T(8,128)(2,1)S(1)}, s32[]{:T(128)}) while((s32[]{:T(128)}, bf16[8,80,3240]{2,1,0:T(8,128)(2,1)}, s32[8,3]{0,1:T(4,128)S(1)}, bf16[8,40,1600]{2,1,0:T(8,128)(2,1)S(1)}, s32[]{:T(128)}) %tuple.120), condition=%wide.while_cond, body=%wide.while_body.sunk | while | flops 2 | bytes 261257 | solution.py:54
  231.8 4.5 pad.269
  236.3 34.0 %while.25 = (s32[]{:T(128)}, f32[8,80,3240]{2,1,0:T(8,128)}, s32[8,3]{0,1:T(4,128)S(1)}, f32[8,40,1600]{2,1,0:T(8,128)}, s32[]{:T(128)}) while((s32[]{:T(128)}, f32[8,80,3240]{2,1,0:T(8,128)}, s32[8,3]{0,1:T(4,128)S(1)}, f32[8,40,1600]{2,1,0:T(8,128)}, s32[]{:T(128)}) %tuple.123), condition=%wide.while_cond.1, body=%wide.while_body.1.sunk | while | flops 2 | bytes 534141 | solution.py:54
  237.0 3.6 dynamic-slice_dynamic-update-slice_fusion.5
  241.2 3.6 dynamic-slice_dynamic-update-slice_fusion.5
  245.5 3.6 dynamic-slice_dynamic-update-slice_fusion.5
  254.0 3.6 dynamic-slice_dynamic-update-slice_fusion.5
  266.7 3.6 dynamic-slice_dynamic-update-slice_fusion.5
  278.1 29.5 %while.24 = (s32[]{:T(128)}, bf16[8,80,3240]{2,1,0:T(8,128)(2,1)}, s32[8,3]{0,1:T(4,128)S(1)}, bf16[8,40,1600]{2,1,0:T(8,128)(2,1)S(1)}, s32[]{:T(128)}) while((s32[]{:T(128)}, bf16[8,80,3240]{2,1,0:T(8,128)(2,1)}, s32[8,3]{0,1:T(4,128)S(1)}, bf16[8,40,1600]{2,1,0:T(8,128)(2,1)S(1)}, s32[]{:T(128)}) %tuple.120), condition=%wide.while_cond, body=%wide.while_body.sunk | while | flops 2 | bytes 261257 | solution.py:54
  322.9 4.5 pad.269
  327.4 34.1 %while.25 = (s32[]{:T(128)}, f32[8,80,3240]{2,1,0:T(8,128)}, s32[8,3]{0,1:T(4,128)S(1)}, f32[8,40,1600]{2,1,0:T(8,128)}, s32[]{:T(128)}) while((s32[]{:T(128)}, f32[8,80,3240]{2,1,0:T(8,128)}, s32[8,3]{0,1:T(4,128)S(1)}, f32[8,40,1600]{2,1,0:T(8,128)}, s32[]{:T(128)}) %tuple.123), condition=%wide.while_cond.1, body=%wide.while_body.1.sunk | while | flops 2 | bytes 534141 | solution.py:54
  328.0 3.6 dynamic-slice_dynamic-update-slice_fusion.5
  332.3 3.6 dynamic-slice_dynamic-update-slice_fusion.5
  336.5 3.6 dynamic-slice_dynamic-update-slice_fusion.5
  340.8 3.6 dynamic-slice_dynamic-update-slice_fusion.5
  357.8 3.6 dynamic-slice_dynamic-update-slice_fusion.5
  364.6 56.1 %all_to_all.5 = f32[2,8,40,1600]{3,2,0,1:T(8,128)S(1)} all-to-all(f32[2,8,40,1600]{3,2,0,1:T(8,128)} %get-tuple-element.134), channel_id=1, replica_groups=mesh['space'=4,'orb'=8] {'orb'}, dimensions={1} | all-to-all | bytes 8192000 | tf_op jit(solution)/shard_map/all_to_all | solution.py:137
  423.9 4.3 reshape_reshape.6
  431.9 22.4 %collective-permute-done.1 = bf16[8,40,1600]{2,1,0:T(8,128)(2,1)S(1)} collective-permute-done((bf16[8,40,1600]{2,1,0:T(8,128)(2,1)}, bf16[8,40,1600]{2,1,0:T(8,128)(2,1)S(1)}, u32[]{:S(2)}, u32[]{:S(2)}) %collective-permute-start.1) | collective-permute-done | bytes 1024032 | tf_op jit(solution)/shard_map/ppermute | solution.py:17
  456.7 4.3 reshape_reshape.7
  (227 shorter events, 163.3 us)
Async XLA Ops:
  6.5 165.4 %copy-start = (bf16[4,40,1600]{2,1,0:T(8,128)(2,1)S(1)}, bf16[4,40,1600]{2,1,0:T(8,128)(2,1)}, u32[]{:S(2)}) copy-start(bf16[4,40,1600]{2,1,0:T(8,128)(2,1)} %param.6) | copy-start | bytes 1536004
  6.5 40.7 %all-gather.2.cloned.1.call-start = ((), (), s32[]{:S(2)}) async-start(), calls=%async_computation.1 | async-start | bytes 4792320 | tf_op jit(solution)/shard_map/all_gather | solution.py:110
  47.2 128.6 %collective-permute-start = (bf16[32,40,1600]{2,1,0:T(8,128)(2,1)}, bf16[32,40,1600]{2,1,0:T(8,128)(2,1)}, u32[]{:S(2)}, u32[]{:S(2)}) collective-permute-start(bf16[32,40,1600]{2,1,0:T(8,128)(2,1)} %all-gather.2.cloned.1.call-done), channel_id=1, source_target_pairs={{8,0},{16,8},{24,16},{0,24},{9,1},{17,9},{25,17},{1,25},{10,2},{18... | collective-permute-start | bytes 12288008 | tf_op jit(solution)/shard_map/ppermute | solution.py:17
  227.5 3.8 slice-start
  230.2 1.1 slice-start.1
  231.8 4.5 copy-start.3
  318.6 3.8 slice-start
  321.2 1.1 slice-start.1
  322.8 4.5 copy-start.3
  420.7 2.0 copy-start.1
  422.7 1.1 copy-start.5
  422.7 1.2 copy-start.4
  423.8 30.5 %collective-permute-start.1 = (bf16[8,40,1600]{2,1,0:T(8,128)(2,1)}, bf16[8,40,1600]{2,1,0:T(8,128)(2,1)S(1)}, u32[]{:S(2)}, u32[]{:S(2)}) collective-permute-start(bf16[8,40,1600]{2,1,0:T(8,128)(2,1)} %fusion.39), channel_id=1, source_target_pairs={{24,0},{0,8},{8,16},{16,24},{25,1},{1,9},{9,17},{17,25},{26,2},{2,... | collective-permute-start | bytes 3072008 | tf_op jit(solution)/shard_map/ppermute | solution.py:17
  428.2 3.6 copy-start.2
Sparse Core Ops, SparseCore 0:
  9.2 37.9 all-gather.1
where the time goes:
time: 481 us; the launch traced here: 473 us
  blocking collectives  175 us (36%)
  local copies, waits for them, and re-layouts  170 us (35%)
  waiting for transfers between devices  63.1 us (13%)
  other arithmetic  42.8 us (9%)
  between operations  13.6 us (3%)
  matrix products  7.02 us (1%)
    gather x96, local copies, waits for them, and re-layouts  127 us
    all_gather x1, blocking collectives, per_device(): lax.all_gather(send_index, ('space', 'orb'), axis=0, tiled=True)  119 us
    all_to_all x1, blocking collectives, per_device(): lax.all_to_all(far_term, 'orb', split_axis=1, concat_axis=1, tiled=True)  56.1 us
    all_gather x1, waiting for transfers between devices, per_device(): members = lax.all_gather(orbitals, 'orb', axis=0, tiled=True)  40 us
    ppermute x2, waiting for transfers between devices, passed_along(): return lax.ppermute(block, axis, route)  22.4 us
    reduce_sum x8, other arithmetic, solve_poisson(): jnp.sum(direction * applied, axis=(1, 2), keepdims=True)  20.7 us
    pad x4, local copies, waits for them, and re-layouts, displace(): jnp.pad(box_values, ((half_side, half_side), (flat_reach, flat_reach)))  15.3 us
  transfers between devices with their start and end apart: 3, of which 2 were waited for; matrix products, arithmetic and copies ran while one was open for 4% of the time, Pallas kernels for 0%

commit v1 on v0

v1 whole, which is shorter than its diff:
```python
import functools

import jax
import jax.numpy as jnp
from jax import lax
from jax.experimental import pallas as pl
from jax.experimental.pallas import tpu as pltpu
from jax.sharding import PartitionSpec as P

B = 40
ITERS = 4
SCREEN = 0.25

GROUPS = 3
TILES = 14
LANES = 128
USED = GROUPS * B
BATCH = 8
PLANE = TILES * BATCH
PLANES = B + 2
MARGIN = 24
ROWS = B + 2 * MARGIN
HALF = B // 2
VMEM_BYTES = 44 * 2**20


def lanes_of(shape):
    return lax.broadcasted_iota(jnp.int32, shape, len(shape) - 1)


def overlaps():
    pieces = []
    for b in range(B):
        group = b // TILES
        for flat in range(b * B // LANES, (b * B + B - 1) // LANES + 1):
            pieces.append((b, flat, b * B - flat * LANES - group * B))
    return pieces


def pack_body(box_ref, table_ref, out_ref):
    count = box_ref.shape[0]
    lane = lanes_of((B, LANES))
    for n in range(count):
        tiles = [jnp.zeros((B, LANES), jnp.float32) for _ in range(TILES)]
        loaded = {}
        for b, flat, shift in overlaps():
            if flat not in loaded:
                width = min(LANES, B * B - flat * LANES)
                part = box_ref[n, :, flat * LANES : flat * LANES + width].astype(jnp.float32)
                if width < LANES:
                    part = jnp.concatenate(
                        [part, jnp.zeros((B, LANES - width), jnp.float32)], axis=1
                    )
                loaded[flat] = part
            first = max(b * B, flat * LANES) - b * B + (b // TILES) * B
            last = min(b * B + B, flat * LANES + LANES) - b * B + (b // TILES) * B
            moved = pltpu.roll(loaded[flat], (-shift) % LANES, axis=1)
            keep = (lane >= first) & (lane < last)
            tiles[b % TILES] = jnp.where(keep, moved, tiles[b % TILES])
        if n == 0:
            tiles[0] = tiles[0] + table_ref[...]
        for t in range(TILES):
            out_ref[n, t] = tiles[t].astype(out_ref.dtype)


def pack(orbitals, table):
    count = orbitals.shape[0]
    return pl.pallas_call(
        pack_body,
        out_shape=jax.ShapeDtypeStruct((count, TILES, B, LANES), jnp.bfloat16),
        in_specs=[pl.BlockSpec(memory_space=pltpu.VMEM)] * 2,
        out_specs=pl.BlockSpec(memory_space=pltpu.VMEM),
        compiler_params=pltpu.CompilerParams(vmem_limit_bytes=VMEM_BYTES),
        name="pack",
    )(orbitals, table)


def finish_body(count, slots, field_ref, near_ref, far_ref, row_ref, out_ref, total):
    lane = lanes_of((B, LANES))
    for n in range(count):
        for t in range(TILES):
            total[n, t] = field_ref[n, t] + far_ref[n, t].astype(jnp.float32)

    def add(j, carry):
        row = row_ref[j]
        for t in range(TILES):
            total[row, t] += near_ref[j, t].astype(jnp.float32)
        return carry

    lax.fori_loop(0, slots, add, 0)
    for n in range(count):
        flats = {}
        for b, flat, shift in overlaps():
            first = max(b * B, flat * LANES) - flat * LANES
            last = min(b * B + B, flat * LANES + LANES) - flat * LANES
            moved = pltpu.roll(total[n, b % TILES], shift % LANES, axis=1)
            keep = (lane >= first) & (lane < last)
            before = flats.get(flat)
            flats[flat] = moved if before is None else jnp.where(keep, moved, before)
        for flat, value in flats.items():
            width = min(LANES, B * B - flat * LANES)
            out_ref[n, :, flat * LANES : flat * LANES + width] = value[:, :width]


def finish(field, near, far, rows):
    count, slots = field.shape[0], near.shape[0]
    vmem = pl.BlockSpec(memory_space=pltpu.VMEM)
    return pl.pallas_call(
        functools.partial(finish_body, count, slots),
        out_shape=jax.ShapeDtypeStruct((count, B, B * B), jnp.float32),
        in_specs=[vmem, vmem, vmem, pl.BlockSpec(memory_space=pltpu.SMEM)],
        out_specs=vmem,
        scratch_shapes=[pltpu.VMEM((count, TILES, B, LANES), jnp.float32)],
        compiler_params=pltpu.CompilerParams(vmem_limit_bytes=VMEM_BYTES),
        name="finish",
    )(field, near, far, rows)


def geometry(offset_ref, left, right, grid_cells):
    shift, live = [], jnp.int32(1)
    for axis in range(3):
        gap = offset_ref[3 * right + axis] - offset_ref[3 * left + axis]
        raw = lax.rem(gap + grid_cells // 2 + grid_cells, grid_cells) - grid_cells // 2
        clipped = jnp.clip(raw, -HALF, HALF)
        live = jnp.where(raw == clipped, live, 0)
        shift.append(clipped)
    return shift, live


def displaced(pad_ref, shift):
    lane = lanes_of((1, LANES))
    group = lane // B
    source_col = lane - group * B - shift[2]
    col_ok = (source_col >= 0) & (source_col < B) & (lane < USED)
    for t in range(TILES):
        index = t - shift[1] + 2 * TILES
        turn = index // TILES - 2
        source = index - (turn + 2) * TILES
        row = TILES * group + t
        source_row = row - shift[1]
        keep = col_ok & (source_row >= 0) & (source_row < B) & (row < B)
        block = pad_ref[source, pl.ds(MARGIN - shift[0], B), :]
        amount = lax.rem(shift[2] - B * turn + 2 * LANES, LANES)
        moved = pltpu.roll(block, amount, axis=1)
        yield t, moved * keep.astype(jnp.float32)


def lockstep(ref, plane, tile):
    return ref[pl.ds(pl.multiple_of(plane * PLANE + tile * BATCH, BATCH), BATCH), :]


def put_lockstep(ref, plane, tile, value):
    ref[pl.ds(pl.multiple_of(plane * PLANE + tile * BATCH, BATCH), BATCH), :] = value


def tree_sum(values):
    while len(values) > 1:
        paired = [a + b for a, b in zip(values[::2], values[1::2])]
        values = paired + ([values[-1]] if len(values) % 2 else [])
    return values[0]


def spread(total):
    return jnp.broadcast_to(jnp.sum(total, axis=1, keepdims=True), (BATCH, LANES))


def solve(directions, residual, image):
    lane = lanes_of((BATCH, LANES))
    column = lane % B
    has_before = (column > 0) & (lane < USED)
    has_after = (column < B - 1) & (lane < USED)
    not_first = lane >= B
    not_last = lane < USED - B
    zero = jnp.zeros((BATCH, LANES), jnp.float32)

    def operator(above, here, below):
        result = []
        for t in range(TILES):
            if t == 0:
                before = jnp.where(not_first, pltpu.roll(here[TILES - 1], B, axis=1), 0.0)
            else:
                before = here[t - 1]
            if t == TILES - 1:
                after = jnp.where(not_last, pltpu.roll(here[0], LANES - B, axis=1), 0.0)
            else:
                after = here[t + 1]
            prior = jnp.where(has_before, pltpu.roll(here[t], 1, axis=1), 0.0)
            following = jnp.where(has_after, pltpu.roll(here[t], LANES - 1, axis=1), 0.0)
            around = (above[t] + below[t]) + (before + after) + (prior + following)
            value = (6.0 + SCREEN) * here[t] - around
            if t == B - TILES * (GROUPS - 1):
                value = jnp.where(not_last, value, 0.0)
            result.append(value)
        return result

    norm = None
    ratio = None
    steps = []
    for k in range(ITERS):
        current = directions[k]
        last = k == ITERS - 1

        def fetch(plane, k=k, ratio=ratio):
            if k == 0:
                return [lockstep(directions[0], plane, t) for t in range(TILES)]
            values = []
            for t in range(TILES):
                value = lockstep(residual, plane, t) + ratio * lockstep(
                    directions[k - 1], plane, t
                )
                put_lockstep(directions[k], plane, t, value)
                values.append(value)
            return values

        def stencil(a, carry, k=k, last=last, fetch=fetch):
            products, squares, above, here = carry
            below = fetch(a + 2)
            applied = operator(above, here, below)
            if not last:
                for t in range(TILES):
                    put_lockstep(image, a + 1, t, applied[t])
            products = products + tree_sum([x * y for x, y in zip(here, applied)])
            if k == 0:
                squares = squares + tree_sum([x * x for x in here])
            return products, squares, here, below

        products, squares, _, _ = lax.fori_loop(
            0, B, stencil, (zero, zero, [zero] * TILES, fetch(1))
        )
        if k == 0:
            norm = spread(squares)
        step = norm / spread(products)
        steps.append(step)
        if last:
            break
        source = directions[0] if k == 0 else residual

        def reduce(a, squares, step=step, source=source):
            values = []
            for t in range(TILES):
                value = lockstep(source, a + 1, t) - step * lockstep(image, a + 1, t)
                put_lockstep(residual, a + 1, t, value)
                values.append(value)
            return squares + tree_sum([x * x for x in values])

        new_norm = spread(lax.fori_loop(0, B, reduce, zero))
        ratio = new_norm / norm
        norm = new_norm

    def combine(a, carry):
        for t in range(TILES):
            parts = [s * lockstep(d, a + 1, t) for s, d in zip(steps, directions)]
            put_lockstep(image, a + 1, t, tree_sum(parts))
        return carry

    lax.fori_loop(0, B, combine, 0)


def clear_edges(refs, pad):
    zero = jnp.zeros((PLANE, LANES), jnp.float32)
    for ref in refs:
        ref[0:PLANE, :] = zero
        ref[(PLANES - 1) * PLANE : PLANES * PLANE, :] = zero
    rim = jnp.zeros((TILES, MARGIN, LANES), jnp.float32)
    pad[:, 0:MARGIN, :] = rim
    pad[:, MARGIN + B : ROWS, :] = rim


def run_batch(slot_of, left_at, right_at, near_to, far_to, scratch):
    shifted, pad, residual, image, *directions = scratch

    def load(j, carry):
        shift, live = slot_of(j)

        @pl.when(live == 1)
        def _():
            for t in range(TILES):
                pad[t, MARGIN : MARGIN + B, :] = right_at(j, t)
            for t, moved in displaced(pad, shift):
                shifted[j, t] = moved
                density = moved * left_at(j, t)
                for k in range(B // 8):
                    start = (8 * k + 1) * PLANE + t * BATCH + j
                    directions[0][pl.ds(start, 8, stride=PLANE), :] = density[8 * k : 8 * k + 8]

        return carry

    lax.fori_loop(0, BATCH, load, 0)
    solve(directions, residual, image)

    def unload(j, carry):
        shift, live = slot_of(j)

        @pl.when(live == 1)
        def _():
            for t in range(TILES):
                rows = []
                for k in range(B // 8):
                    start = (8 * k + 1) * PLANE + t * BATCH + j
                    rows.append(image[pl.ds(start, 8, stride=PLANE), :])
                potential = jnp.concatenate(rows, axis=0)
                if near_to is not None:
                    near_to(j, t, potential * shifted[j, t])
                if far_to is not None:
                    pad[t, MARGIN : MARGIN + B, :] = potential * left_at(j, t)
            if far_to is not None:
                for t, moved in displaced(pad, [-s for s in shift]):
                    far_to(j, t, moved)

        if near_to is not None:
            near_to(j, None, live)
        return carry

    lax.fori_loop(0, BATCH, unload, 0)


def batch_scratch():
    lock = pltpu.VMEM((PLANES * PLANE, LANES), jnp.float32)
    return [
        pltpu.VMEM((BATCH, TILES, B, LANES), jnp.float32),
        pltpu.VMEM((TILES, ROWS, LANES), jnp.float32),
    ] + [lock] * (2 + ITERS)


def clear_lockstep(ref):
    def one(a, carry):
        ref[pl.ds(pl.multiple_of(a * PLANE, PLANE), PLANE), :] = jnp.zeros(
            (PLANE, LANES), jnp.float32
        )
        return carry

    lax.fori_loop(0, PLANES, one, 0)


def forward_body(
    count, grid_cells, where_ref, offset_ref, left_ref, right_ref, boxes, incoming,
    near_ref, far_ref, far_sum, *scratch,
):
    slots = near_ref.shape[0]
    first_left, first_right = where_ref[0], where_ref[1]
    clear_edges(scratch[2:], scratch[1])
    clear_lockstep(scratch[4])
    for n in range(count):
        for t in range(TILES):
            far_sum[n, t] = jnp.zeros((B, LANES), jnp.float32)

    def batch(i, carry):
        def rows(j):
            return (i * BATCH + j) * count + left_ref[i * BATCH + j], right_ref[i * BATCH + j]

        def slot_of(j):
            left, right = rows(j)
            return geometry(offset_ref, first_left + left, first_right + right, grid_cells)

        def near_to(j, t, value):
            if t is not None:
                near_ref[i * BATCH + j, t] = value.astype(near_ref.dtype)
            else:

                @pl.when(value == 0)
                def _():
                    near_ref[i * BATCH + j] = jnp.zeros((TILES, B, LANES), near_ref.dtype)

        def far_to(j, t, value):
            far_sum[rows(j)[1], t] += value

        run_batch(
            slot_of,
            lambda j, t: boxes[rows(j)[0], t].astype(jnp.float32),
            lambda j, t: incoming[rows(j)[1], t].astype(jnp.float32),
            near_to, far_to, scratch,
        )
        return carry

    lax.fori_loop(0, slots // BATCH, batch, 0)
    for n in range(count):
        for t in range(TILES):
            far_ref[n, t] = far_sum[n, t].astype(far_ref.dtype)


def forward_pairs(where, offsets, left, right, boxes, incoming, grid_cells):
    slots, count = left.shape[0], incoming.shape[0]
    vmem, smem = (pl.BlockSpec(memory_space=m) for m in (pltpu.VMEM, pltpu.SMEM))
    shape = (TILES, B, LANES)
    return pl.pallas_call(
        functools.partial(forward_body, count, grid_cells),
        out_shape=(
            jax.ShapeDtypeStruct((slots,) + shape, jnp.bfloat16),
            jax.ShapeDtypeStruct((count,) + shape, jnp.bfloat16),
        ),
        in_specs=[smem] * 4 + [vmem] * 2,
        out_specs=(vmem, vmem),
        scratch_shapes=[pltpu.VMEM((count,) + shape, jnp.float32)] + batch_scratch(),
        compiler_params=pltpu.CompilerParams(vmem_limit_bytes=VMEM_BYTES),
        name="forward_pairs",
    )(where, offsets, left, right, boxes, incoming)


def group_body(
    count, grid_cells, where_ref, offset_ref, mine_ref, theirs_ref, sent_ref, lefts_ref,
    boxes, field, *scratch,
):
    slots = mine_ref.shape[0]
    first, mine = where_ref[0], where_ref[1]
    clear_edges(scratch[2:], scratch[1])
    clear_lockstep(scratch[4])
    for n in range(count):
        for t in range(TILES):
            field[n, t] = jnp.zeros((B, LANES), jnp.float32)

    def batch(i, carry):
        def run(left_of, right_of, near, far):
            def slot_of(j):
                return geometry(offset_ref, first + left_of(j), first + right_of(j), grid_cells)

            run_batch(
                slot_of,
                lambda j, t: boxes[left_of(j), t].astype(jnp.float32),
                lambda j, t: boxes[right_of(j), t].astype(jnp.float32),
                near, far, scratch,
            )

        def near_to(j, t, value):
            if t is not None:
                field[mine_ref[i * BATCH + j], t] += value

        def far_to(j, t, value):
            field[sent_ref[i * BATCH + j], t] += value

        run(
            lambda j: mine + mine_ref[i * BATCH + j],
            lambda j: (i * BATCH + j) * count + theirs_ref[i * BATCH + j],
            near_to, None,
        )
        run(
            lambda j: (i * BATCH + j) * count + lefts_ref[i * BATCH + j],
            lambda j: mine + sent_ref[i * BATCH + j],
            None, far_to,
        )
        return carry

    lax.fori_loop(0, slots // BATCH, batch, 0)


def group_pairs(where, offsets, mine, theirs, sent, lefts, boxes, count, grid_cells):
    vmem, smem = (pl.BlockSpec(memory_space=m) for m in (pltpu.VMEM, pltpu.SMEM))
    return pl.pallas_call(
        functools.partial(group_body, count, grid_cells),
        out_shape=jax.ShapeDtypeStruct((count, TILES, B, LANES), jnp.float32),
        in_specs=[smem] * 6 + [vmem],
        out_specs=vmem,
        scratch_shapes=batch_scratch(),
        compiler_params=pltpu.CompilerParams(vmem_limit_bytes=VMEM_BYTES),
        name="group_pairs",
    )(where, offsets, mine, theirs, sent, lefts, boxes)


def along_space(block, distance):
    size = lax.axis_size("space")
    return lax.ppermute(block, "space", [((i - distance) % size, i) for i in range(size)])


def per_device(orbitals, box_offset, send_index, pair_left):
    count = orbitals.shape[0]
    spaces, orbs = lax.axis_size("space"), lax.axis_size("orb")
    grid_cells = spaces * HALF
    space, orb = lax.axis_index("space"), lax.axis_index("orb")
    group_first = space * orbs * count
    offsets = box_offset.reshape(-1)

    free = LANES - USED
    entries = jnp.concatenate([send_index[0].reshape(-1), pair_left[0].reshape(-1)])
    lines = 4 * orbs // free
    table = jnp.pad(
        entries.astype(jnp.float32).reshape(lines, free), ((0, B - lines), (USED, 0))
    )
    packed = pack(orbitals, table)

    incoming = along_space(packed, -1)
    boxes = lax.all_gather(packed, "orb", axis=0, tiled=True)

    def tables(block):
        lead = block.reshape((-1, count) + block.shape[1:])[:, 0, 0, :lines, USED:]
        return lead.astype(jnp.int32).reshape(-1, 2, 2, orbs)

    group = tables(boxes)
    sent_here = jnp.take(group[:, 0, 0, :], orb, axis=1)
    lefts_here = jnp.take(group[:, 1, :, :], orb, axis=2)
    next_sent = tables(incoming)[0, 0, 1]

    next_first = ((space + 1) % spaces * orbs + orb) * count
    near, far = forward_pairs(
        jnp.stack([group_first, next_first]), offsets, lefts_here[:, 1], next_sent,
        boxes, incoming, grid_cells,
    )
    near = lax.all_to_all(near, "orb", split_axis=0, concat_axis=0, tiled=True)
    far = along_space(far, 1)
    field = group_pairs(
        jnp.stack([group_first, orb * count]), offsets, pair_left[0, 0], sent_here,
        send_index[0, 0], lefts_here[:, 0], boxes, count, grid_cells,
    )
    return finish(field, near, far, pair_left[0, 1])


def solution(mesh):
    split = P(("space", "orb"), None, None)
    return jax.shard_map(
        per_device, mesh=mesh, in_specs=(split, P(), split, split), out_specs=split,
        check_vma=False,
    )
```

time: 481 us -> 147 us (0.31); the launches traced: 473 us -> 146 us
  blocking collectives: 175 us -> 0 us
  local copies, waits for them, and re-layouts: 170 us -> 6.95 us
  Pallas kernels: 0 us -> 76 us
  other arithmetic: 42.8 us -> 1.29 us
  waiting for transfers between devices: 63.1 us -> 38.5 us
  starting transfers between devices: 0.55 us -> 9.71 us
  matrix products: 7.02 us -> 0 us
    gather x104 -> x0, local copies, waits for them, and re-layouts: 137 us -> none
    all_gather x1 -> x0, blocking collectives: 119 us -> none  [per_device(): lax.all_gather(send_index, ('space', 'orb'), axis=0, tiled=True)]
    pallas_call x0 -> x4, Pallas kernels: none -> 76 us  [the longest x1 48.6 us: group_pairs(): pl.pallas_call(functools.partial(group_body, count, grid_cells), out_shap...]
    all_to_all x1 -> x0, blocking collectives: 56.1 us -> none  [per_device(): lax.all_to_all(far_term, 'orb', split_axis=1, concat_axis=1, tiled=True)]
    reduce_sum x14 -> x0, other arithmetic: 24.1 us -> none  [the longest x8 20.7 us: solve_poisson(): jnp.sum(direction * applied, axis=(1, 2), keepdims=True)]
    all_gather x1, waiting for transfers between devices: 40 us -> 24.4 us  [per_device(): boxes = lax.all_gather(packed, 'orb', axis=0, tiled=True)]
    pad x4 -> x1, local copies, waits for them, and re-layouts: 15.3 us -> 0.08 us  [per_device(): jnp.pad(entries.astype(jnp.float32).reshape(lines, free), ((0, B - lines)...]
    another operation x3 -> x0, local copies, waits for them, and re-layouts: 9.31 us -> none  [the longest x2 8.55 us: collect_terms(): flat_terms = terms.reshape(terms.shape[0], -1)]
  transfers between devices with their start and end apart: 3 -> 4, of which waited for: 2 -> 2; matrix products, arithmetic and copies ran while one was open for 4% -> 1% of each run, Pallas kernels for 0% -> 33%
where the time goes in v1:
time: 147 us; the launch traced here: 146 us
  Pallas kernels  76 us (52%)
  waiting for transfers between devices  38.5 us (26%)
  between operations  13.5 us (9%)
  starting transfers between devices  9.71 us (7%)
  local copies, waits for them, and re-layouts  6.95 us (5%)
    pallas_call x1, Pallas kernels, group_pairs(): pl.pallas_call(functools.partial(group_body, count, grid_cells), out_shap...  48.6 us
    all_gather x1, waiting for transfers between devices, per_device(): boxes = lax.all_gather(packed, 'orb', axis=0, tiled=True)  24.4 us
    pallas_call x1, Pallas kernels, forward_pairs(): pl.pallas_call(functools.partial(forward_body, count, grid_cells), out_sh...  23.3 us
    ppermute x2, waiting for transfers between devices, along_space(): lax.ppermute(block, 'space', [((i - distance) % size, i) for i in range(s...  14.1 us
    unnamed x14, local copies, waits for them, and re-layouts  5.77 us
    all_to_all x1, starting transfers between devices, per_device(): near = lax.all_to_all(near, 'orb', split_axis=0, concat_axis=0, tiled=True)  5.28 us
    ppermute x2, starting transfers between devices, along_space(): lax.ppermute(block, 'space', [((i - distance) % size, i) for i in range(s...  4.43 us
  transfers between devices with their start and end apart: 4, of which 2 were waited for; matrix products, arithmetic and copies ran while one was open for 1% of the time, Pallas kernels for 33%

profile of v1, /device:TPU:12, one launch (start us, length us, event | category | flops | bytes accessed | tf_op | source)
XLA Modules:
  0.0 145.9 jit_solution(12740197296126711878)
XLA Ops:
  6.5 0.7 add_convert_fusion
  7.3 0.1 pad.4.table_ref
  7.3 1.0 copy-done.2
  8.4 1.4 pack.1
  9.7 0.0 all-gather.2.cloned.1.call-update
  9.8 0.5 collective-permute-start
  10.3 0.1 copy.12
  10.4 0.2 reshape.35.offset_ref
  10.6 0.1 pad_add_fusion.1.where_ref
  10.7 14.1 %collective-permute-done.incoming = bf16[4,14,40,128]{3,2,1,0:T(8,128)(2,1)S(1)} collective-permute-done((bf16[4,14,40,128]{3,2,1,0:T(8,128)(2,1)}, bf16[4,14,40,128]{3,2,1,0:T(8,128)(2,1)S(1)}, u32[]{:S(2)}, u32[]{:S(2)}) %collective-permute-start) | collective-permute-done | bytes 573472 | tf_op jit(solution)/shard_map/ppermute | solution.py:460
  24.8 0.1 slice.60
  24.8 24.4 %all-gather.2.cloned.1.call-done.boxes = bf16[32,14,40,128]{3,2,1,0:T(8,128)(2,1)} async-done(((bf16[4,14,40,128]{3,2,1,0:T(8,128)(2,1)}), bf16[32,14,40,128]{3,2,1,0:T(8,128)(2,1)}) %all-gather.2.cloned.1.call-update) | async-done | bytes 4587536 | tf_op jit(solution)/shard_map/all_gather | solution.py:480
  49.2 0.8 slice.57
  50.1 0.2 select_reduce_fusion
  50.3 2.3 %copy-done = bf16[32,14,40,128]{3,2,1,0:T(8,128)(2,1)S(1)} copy-done((bf16[32,14,40,128]{3,2,1,0:T(8,128)(2,1)S(1)}, bf16[32,14,40,128]{3,2,1,0:T(8,128)(2,1)}, u32[]{:S(2)}) %copy-start) | copy-done | bytes 4587544
  52.6 23.3 %forward_pairs.1 = (bf16[8,14,40,128]{3,2,1,0:T(8,128)(2,1)}, bf16[4,14,40,128]{3,2,1,0:T(8,128)(2,1)S(1)}) custom-call(s32[2]{0:T(128)S(1)} %pad_add_fusion.1.where_ref, s32[384]{0:T(512)S(1)} %reshape.35.offset_ref, s32[8]{0:T(128)S(1)} %get-tuple-element.33.left_ref, s32[8]{0:T(128)S(1)} %fusion.right_ref, bf16[32,14,40,128]{3,2,1,0:T(8,128)(2,1)S(1)} %copy-done, ...), custom_call_target="tpu_custom_call" | custom-call | tf_op jit(solution)/shard_map/forward_pairs/pallas_call | solution.py:385
  75.9 5.3 %all-to-all-start = ((bf16[8,14,40,128]{3,2,1,0:T(8,128)(2,1)}), bf16[8,14,40,128]{3,2,1,0:T(8,128)(2,1)S(1)}, u32[]{:S(2)}, u32[]{:S(2)}) async-start(bf16[8,14,40,128]{3,2,1,0:T(8,128)(2,1)} %get-tuple-element.7), calls=%async_computation | async-start | bytes 2293760 | tf_op jit(solution)/shard_map/all_to_all | solution.py:496
  81.2 3.9 %collective-permute-start.1 = (bf16[4,14,40,128]{3,2,1,0:T(8,128)(2,1)S(1)}, bf16[4,14,40,128]{3,2,1,0:T(8,128)(2,1)S(1)}, u32[]{:S(2)}, u32[]{:S(2)}) collective-permute-start(bf16[4,14,40,128]{3,2,1,0:T(8,128)(2,1)S(1)} %get-tuple-element.8), channel_id=1, source_target_pairs={{24,0},{0,8},{8,16},{16,24},{25,1},{1,9},{9,17},{17,25},{26,2},{2,... | collective-permute-start | bytes 1720328 | tf_op jit(solution)/shard_map/ppermute | solution.py:460
  85.1 0.1 pad_add_fusion.where_ref
  85.2 0.2 select_reduce_fusion.1.theirs_ref
  85.4 2.3 %copy-done.1 = bf16[32,14,40,128]{3,2,1,0:T(8,128)(2,1)S(1)} copy-done((bf16[32,14,40,128]{3,2,1,0:T(8,128)(2,1)S(1)}, bf16[32,14,40,128]{3,2,1,0:T(8,128)(2,1)}, u32[]{:S(2)}) %copy-start.1) | copy-done | bytes 4587544
  87.7 48.6 %group_pairs.1.field_ref = f32[4,14,40,128]{3,2,1,0:T(8,128)S(1)} custom-call(s32[2]{0:T(128)S(1)} %pad_add_fusion.where_ref, s32[384]{0:T(512)S(1)} %reshape.35.offset_ref, s32[8]{0:T(128)S(1)} %get-tuple-element.32.mine_ref, s32[8]{0:T(128)S(1)} %select_reduce_fusion.1.theirs_ref, s32[8]{0:T(128)S(1)} %get-tuple-element.35.sent_ref, ...), custom_call_target="tpu_custom_call" | custom-call | tf_op jit(solution)/shard_map/group_pairs/pallas_call | solution.py:447
  136.3 0.0 all-to-all-done.near_ref
  136.3 2.7 %finish.1 = f32[4,40,1600]{2,1,0:T(8,128)} custom-call(f32[4,14,40,128]{3,2,1,0:T(8,128)S(1)} %group_pairs.1.field_ref, bf16[8,14,40,128]{3,2,1,0:T(8,128)(2,1)S(1)} %all-to-all-done.near_ref, bf16[4,14,40,128]{3,2,1,0:T(8,128)(2,1)S(1)} %collective-permute-done.1.far_ref, s32[8]{0:T(128)S(1)} %get-tuple-element.31.row_ref), custom_call_target="tpu_custom_call" | custom-call | tf_op jit(solution)/shard_map/finish/pallas_call | solution.py:108
  (18 shorter events, 0.1 us)
Async XLA Ops:
  6.5 3.7 %copy-start.5 = (s32[128,3]{0,1:T(4,128)S(1)}, s32[128,3]{0,1:T(4,128)}, u32[]{:S(2)}) copy-start(s32[128,3]{0,1:T(4,128)} %param.5) | copy-start | bytes 4612
  6.5 42.7 %all-gather.2.cloned.1.call-start = ((), (), s32[]{:S(2)}) async-start(), calls=%async_computation.1 | async-start | bytes 5160960 | tf_op jit(solution)/shard_map/all_gather | solution.py:480
  7.3 1.0 copy-start.2
  9.8 15.0 %collective-permute-start = (bf16[4,14,40,128]{3,2,1,0:T(8,128)(2,1)}, bf16[4,14,40,128]{3,2,1,0:T(8,128)(2,1)S(1)}, u32[]{:S(2)}, u32[]{:S(2)}) collective-permute-start(bf16[4,14,40,128]{3,2,1,0:T(8,128)(2,1)} %pack.1), channel_id=1, source_target_pairs={{8,0},{16,8},{24,16},{0,24},{9,1},{17,9},{25,17},{1,25},{10,2},{18... | collective-permute-start | bytes 1720328 | tf_op jit(solution)/shard_map/ppermute | solution.py:460
  50.3 2.3 %copy-start = (bf16[32,14,40,128]{3,2,1,0:T(8,128)(2,1)S(1)}, bf16[32,14,40,128]{3,2,1,0:T(8,128)(2,1)}, u32[]{:S(2)}) copy-start(bf16[32,14,40,128]{3,2,1,0:T(8,128)(2,1)} %all-gather.2.cloned.1.call-done.boxes) | copy-start | bytes 13762564
  75.9 9.3 %copy-start.3 = (s32[1,2,8]{2,1,0:T(2,128)S(1)}, s32[1,2,8]{2,1,0:T(2,128)}, u32[]{:S(2)}) copy-start(s32[1,2,8]{2,1,0:T(2,128)} %param.7) | copy-start | bytes 196
  75.9 9.3 %copy-start.4 = (s32[1,2,8]{2,1,0:T(2,128)S(1)}, s32[1,2,8]{2,1,0:T(2,128)}, u32[]{:S(2)}) copy-start(s32[1,2,8]{2,1,0:T(2,128)} %param.6) | copy-start | bytes 196
  75.9 60.4 %all-to-all-start = ((bf16[8,14,40,128]{3,2,1,0:T(8,128)(2,1)}), bf16[8,14,40,128]{3,2,1,0:T(8,128)(2,1)S(1)}, u32[]{:S(2)}, u32[]{:S(2)}) async-start(bf16[8,14,40,128]{3,2,1,0:T(8,128)(2,1)} %get-tuple-element.7), calls=%async_computation | async-start | bytes 2293760 | tf_op jit(solution)/shard_map/all_to_all | solution.py:496
  81.2 55.1 %collective-permute-start.1 = (bf16[4,14,40,128]{3,2,1,0:T(8,128)(2,1)S(1)}, bf16[4,14,40,128]{3,2,1,0:T(8,128)(2,1)S(1)}, u32[]{:S(2)}, u32[]{:S(2)}) collective-permute-start(bf16[4,14,40,128]{3,2,1,0:T(8,128)(2,1)S(1)} %get-tuple-element.8), channel_id=1, source_target_pairs={{24,0},{0,8},{8,16},{16,24},{25,1},{1,9},{9,17},{17,25},{26,2},{2,... | collective-permute-start | bytes 1720328 | tf_op jit(solution)/shard_map/ppermute | solution.py:460
  85.4 2.3 %copy-start.1 = (bf16[32,14,40,128]{3,2,1,0:T(8,128)(2,1)S(1)}, bf16[32,14,40,128]{3,2,1,0:T(8,128)(2,1)}, u32[]{:S(2)}) copy-start(bf16[32,14,40,128]{3,2,1,0:T(8,128)(2,1)} %all-gather.2.cloned.1.call-done.boxes) | copy-start | bytes 13762564
Sparse Core Ops, SparseCore 0:
  9.9 39.2 all-gather.1
